TPU v7x, 32 devices: a whole 2x2x4 slice. The times are simulated.
32 devices in a mesh: seq: 16 (over z, y, x), head: 2 (over core).
Axes of the slice: x: 2, y: 2, z: 4, core: 2. Of those that a mesh axis runs over, the one named last changes fastest.
Arguments:
- queries: bfloat16 [2048, 4096], P('seq', 'head'), may hold values from -6 to 6
- keys: bfloat16 [2048, 4096], P('seq', 'head'), may hold values from -6 to 6
- values: bfloat16 [2048, 4096], P('seq', 'head'), may hold values from -6 to 6
- log_decay: float32 [2048, 32], P('seq', 'head'), may hold values from -0.75 to 0
- norm_gain: float32 [4096], P('head'), may hold values from 0.1 to 1.9
- out_weight: bfloat16 [4096, 4096], P('head'), may hold values from -0.125 to 0.125
- steer_ids: int32 [2048], P('seq'), may hold values from 0 to 15
- steer_table: bfloat16 [16, 4096], P(None, 'head'), may hold values from -3 to 3
Outputs:
- layer_out: bfloat16 [2048, 4096], P('seq', 'head')
All inputs are finite; a program needn't handle non-finite values.
Results may differ from a plain program's by a relative error of at most 0.0052.
Values sent between devices are 32-bit elements; how exact they have to be, the bound alone decides.
A program may use at most 64 MiB of HBM per device.

v0:
```python
import jax
import jax.numpy as jnp
from jax import lax
from jax.sharding import PartitionSpec as P

SPAN = 128


def prefix(part, axis, combine, identity):
    place = lax.axis_index(axis)
    gathered = jax.tree.map(lambda a: lax.all_gather(a, axis), part)
    state = jax.tree.map(lambda a, e: jnp.zeros_like(a) + jnp.asarray(e, a.dtype), part, identity)

    def one(step, state):
        return combine(
            state, jax.tree.map(lambda a: lax.dynamic_index_in_dim(a, step, 0, False), gathered)
        )

    return lax.fori_loop(0, place, one, state)


def block_step(state, inputs):
    query, key_blk, value_blk, decay = inputs
    cum = jnp.cumsum(decay, axis=1)
    size = decay.shape[1]
    rows = lax.broadcasted_iota(jnp.int32, (size, size), 0)
    cols = lax.broadcasted_iota(jnp.int32, (size, size), 1)
    lower = (cols <= rows)[None]
    scores = jnp.einsum("hte,hse->hts", query, key_blk, preferred_element_type=jnp.float32)
    diffs = jnp.where(lower, cum[:, :, None] - cum[:, None, :], 0.0)
    block_weights = (jnp.where(lower, jnp.exp(diffs), 0.0) * scores).astype(jnp.bfloat16)
    intra = jnp.einsum("hts,hse->hte", block_weights, value_blk, preferred_element_type=jnp.float32)
    inter = jnp.exp(cum)[:, :, None] * jnp.einsum(
        "hte,hef->htf", query.astype(jnp.float32), state, precision=lax.Precision.HIGHEST
    )
    total = cum[:, -1]
    scaled_keys = key_blk.astype(jnp.float32) * jnp.exp(total[:, None] - cum)[:, :, None]
    update = jnp.einsum(
        "hse,hsf->hef", scaled_keys, value_blk.astype(jnp.float32), precision=lax.Precision.HIGHEST
    )
    new_state = jnp.exp(total)[:, None, None] * state + update
    return (new_state, intra + inter)


def join_memory(earlier, later):
    return (earlier[0] + later[0], jnp.exp(later[0])[:, None, None] * earlier[1] + later[1])


def shards(queries, keys, values, log_decay, norm_gain, out_weight, steer_ids, steer_table):
    tok_rows, features = queries.shape
    heads_here = log_decay.shape[1]
    head_size = features // heads_here
    count = tok_rows // SPAN

    def split(array):
        return array.reshape(count, SPAN, heads_here, head_size).transpose(0, 2, 1, 3)

    decays = log_decay.reshape(count, SPAN, heads_here).transpose(0, 2, 1)
    start = jnp.zeros((heads_here, head_size, head_size), jnp.float32)
    local_memory, blocks = lax.scan(
        block_step, start, (split(queries), split(keys), split(values), decays)
    )
    device_log = jnp.sum(log_decay, axis=0)
    identity = (jnp.zeros((heads_here,), jnp.float32), start)
    passed = prefix((device_log, local_memory), "seq", join_memory, identity)
    earlier_memory = passed[1]
    running = jnp.cumsum(log_decay, axis=0)
    query_heads = queries.reshape(tok_rows, heads_here, head_size).astype(jnp.float32)
    carried = jnp.exp(running)[:, :, None] * jnp.einsum(
        "the,hef->thf", query_heads, earlier_memory, precision=lax.Precision.HIGHEST
    )
    attended = blocks.transpose(0, 2, 1, 3).reshape(tok_rows, heads_here, head_size) + carried
    mean_sq = jnp.mean(attended * attended, axis=-1, keepdims=True)
    normed = (attended * lax.rsqrt(mean_sq + 1e-06)).reshape(tok_rows, features) * norm_gain
    normed = normed.astype(jnp.bfloat16)
    partial_term = jnp.dot(normed, out_weight, preferred_element_type=jnp.float32)
    onehot = (
        steer_ids[:, None] == jnp.arange(steer_table.shape[0], dtype=jnp.int32)[None, :]
    ).astype(jnp.bfloat16)
    steering = jnp.dot(onehot, steer_table, preferred_element_type=jnp.float32)
    whole_sum = lax.psum(partial_term, "head")
    column_width = steer_table.shape[1]
    summed = lax.dynamic_slice_in_dim(
        whole_sum, lax.axis_index("head") * column_width, column_width, 1
    )
    return (summed + steering).astype(jnp.bfloat16)


def solution(mesh):
    in_specs = (
        P("seq", "head"),
        P("seq", "head"),
        P("seq", "head"),
        P("seq", "head"),
        P("head"),
        P("head", None),
        P("seq"),
        P(None, "head"),
    )
    out_specs = P("seq", "head")
    return jax.shard_map(shards, mesh=mesh, in_specs=in_specs, out_specs=out_specs, check_vma=False)
```

profile of v0, /device:TPU:25, one launch (start us, length us, event | category | flops | bytes accessed | tf_op | source)
XLA Modules:
  0.0 269.6 jit_solution(12327497487724483794)
XLA Ops:
  6.5 1.0 reduce_window_sum.23
  7.9 1.2 copy.46
  9.0 1.3 copy.41
  10.3 1.7 convolution_add_fusion.1
  12.1 0.8 reduce_sum.18
  12.9 0.8 copy.33
  13.7 1.2 dynamic-slice.5
  15.7 0.2 dynamic-update-slice
  15.9 28.6 %all-reduce = f32[256]{0:T(256)S(1)} all-reduce(f32[256]{0:T(256)S(1)} %dynamic-update-slice), channel_id=2, replica_groups=mesh['seq'=16,'head'=2] {'seq'}, use_global_device_ids=true, to_apply=%add | all-reduce | flops 256 | bytes 2048
  44.8 1.2 copy.45
  46.0 0.8 bitcast_bitcast_fusion
  46.9 1.8 fusion.7
  48.7 155.0 %all-gather.4.cloned.1.call-done = f32[256,128,128]{2,1,0:T(8,128)} async-done(((f32[16,128,128]{2,1,0:T(8,128)}), f32[256,128,128]{2,1,0:T(8,128)}) %all-gather.4.cloned.1.call-update) | async-done | bytes 16777232 | tf_op jit(solution)/shard_map/all_gather | solution.py:11
  203.8 18.0 %while.3 = (s32[]{:T(128)}, f32[16,128,128]{2,1,0:T(8,128)S(1)}, s32[]{:T(128)}, f32[16,16]{1,0:T(8,128)S(1)}, f32[16,16,128,128]{3,2,1,0:T(8,128)}, /*index=5*/s32[]{:T(128)}, s32[]{:T(128)}, s32[]{:T(128)}) while((s32[]{:T(128)}, f32[16,128,128]{2,1,0:T(8,128)S(1)}, s32[]{:T(128)}, f32[16,16]{1,0:T(8,128)S(1)}, ...), condition=%wide.region_4.5_spmd, body=%wide.region_3.4_spmd.sunk | while | flops 524293 | bytes 3146047 | solution.py:19
  203.8 1.4 bitcast_add_fusion.2
  205.3 1.4 bitcast_add_fusion.2
  206.8 1.4 bitcast_add_fusion.2
  208.3 1.4 bitcast_add_fusion.2
  209.8 1.4 bitcast_add_fusion.2
  211.3 1.4 bitcast_add_fusion.2
  212.8 1.4 bitcast_add_fusion.2
  214.3 1.4 bitcast_add_fusion.2
  215.8 1.4 bitcast_add_fusion.2
  217.3 1.4 bitcast_add_fusion.2
  218.8 1.4 bitcast_add_fusion.2
  220.3 1.4 bitcast_add_fusion.2
  221.8 1.0 fusion.5
  222.8 1.2 multiply_reduce_fusion
  224.2 0.3 fusion.8
  224.5 9.5 %fusion.36 = f32[128,4096]{1,0:T(8,128)} fusion(bf16[128,2048]{0,1:T(8,128)(2,1)S(1)} %fusion.8, bf16[2048,4096]{1,0:T(8,128)(2,1)} %param.15), kind=kOutput, calls=%fused_computation.51 | convolution fusion | flops 2147483648 | bytes 19398656 | tf_op jit(solution)/shard_map/dot_general | solution.py:76
  234.0 26.4 %all-reduce.3.cloned.1.call-done = f32[128,4096]{1,0:T(8,128)} async-done(((f32[128,4096]{1,0:T(8,128)}), f32[128,4096]{1,0:T(8,128)}) %all-reduce.3.cloned.1.call-update) | async-done | bytes 2097168 | tf_op jit(solution)/shard_map/psum | solution.py:81
  260.4 2.4 fusion
  (36 shorter events, 1.0 us)
Async XLA Ops:
  6.5 253.9 %copy-start = (bf16[16,2048]{1,0:T(8,128)(2,1)S(1)}, bf16[16,2048]{1,0:T(8,128)(2,1)}, u32[]{:S(2)}) copy-start(bf16[16,2048]{1,0:T(8,128)(2,1)} %param.17) | copy-start | bytes 196612
  6.5 215.3 %copy-start.1 = (bf16[128,2048]{1,0:T(8,128)(2,1)S(1)}, bf16[128,2048]{1,0:T(8,128)(2,1)}, u32[]{:S(2)}) copy-start(bf16[128,2048]{1,0:T(8,128)(2,1)} %param.10) | copy-start | bytes 1572868
  6.5 197.1 %all-gather.4.cloned.1.call-start = ((), (), s32[]{:S(2)}) async-start(), calls=%async_computation.1 | async-start | bytes 17825792 | tf_op jit(solution)/shard_map/all_gather | solution.py:11
  12.1 212.1 %copy-start.2 = (f32[2048]{0:T(1024)S(1)}, f32[2048]{0:T(1024)}, u32[]{:S(2)}) copy-start(f32[2048]{0:T(1024)} %param.14) | copy-start | bytes 24580
  12.1 248.3 %all-reduce.3.cloned.1.call-start = ((), (), s32[]{:S(2)}) async-start(), calls=%async_computation | async-start | bytes 4194304 | tf_op jit(solution)/shard_map/psum | solution.py:81
  222.8 37.6 %copy-start.3 = (s32[128]{0:T(128)S(1)}, s32[128]{0:T(128)}, u32[]{:S(2)}) copy-start(s32[128]{0:T(128)} %param.16) | copy-start | bytes 1540
Sparse Core Ops, SparseCore 0:
  12.2 191.4 all-gather.3
  234.1 26.2 all-reduce.2
where the time goes:
time: 272 us; the launch traced here: 270 us
  waiting for transfers between devices  181 us (67%)
  blocking collectives  28.6 us (11%)
  other arithmetic  19.9 us (7%)
  matrix products  17.6 us (6%)
  between operations  14.2 us (5%)
  local copies, waits for them, and re-layouts  7.35 us (3%)
    all_gather x1, waiting for transfers between devices, prefix(): gathered = jax.tree.map(lambda a: lax.all_gather(a, axis), part)  155 us
    unnamed x1, blocking collectives  28.6 us
    psum x1, waiting for transfers between devices, shards(): whole_sum = lax.psum(partial_term, 'head')  26.4 us
    add x12, other arithmetic, join_memory(): jnp.exp(later[0])[:, None, None] * earlier[1] + later[1]  17.4 us
    dot_general x1, matrix products, shards(): jnp.dot(normed, out_weight, preferred_element_type=jnp.float32)  9.45 us
  transfers between devices with their start and end apart: 2, of which 2 were waited for; matrix products, arithmetic and copies ran while one was open for 3% of the time, Pallas kernels for 0%

commit v1 on v0

v1 whole, which is shorter than its diff:
```python
import functools

import jax
import jax.numpy as jnp
from jax import lax
from jax.experimental import pallas as pl
from jax.experimental.pallas import tpu as pltpu
from jax.sharding import PartitionSpec as P

MESH = pl.DeviceIdType.MESH
F32 = jnp.float32
BF16 = jnp.bfloat16
W_COPIES = 8


def split_high_low(x):
    high = x.astype(BF16)
    return high, (x - high.astype(F32)).astype(BF16)


def kernel(
    n, nh, G, SUB, hb, nt,
    q_ref, k_ref, v_ref, ld_ref, gain_ref, w_hbm, ids_ref, tab_ref,
    out_ref,
    w_ref, mem_own, dec_own, mem_in, dec_in, chain_out, chain_in, pre_out, pre_in,
    intra, ecb, acc, xout, xin,
    w_sem, mem_s, mem_r, dec_s, dec_r, ch_s, ch_r, pre_s, pre_r, x_s, x_r,
):
    T, features = q_ref.shape
    HD = 128
    heads = features // HD
    HS = heads // G
    NG = n // G
    width = w_hbm.shape[1]
    CW = width // nh
    TW = CW // nt
    s = lax.axis_index("seq")
    e = lax.axis_index("head")
    g = s // G
    c = s % G

    def member(o):
        return (c + o) % G

    barrier = pltpu.get_barrier_semaphore()
    for o in range(1, G):
        pl.semaphore_signal(barrier, 1, device_id=(g * G + member(o), e), device_id_type=MESH)
    for o in range(1, nh):
        pl.semaphore_signal(barrier, 1, device_id=(s, (e + o) % nh), device_id_type=MESH)

    @pl.when(g > 0)
    def _():
        pl.semaphore_signal(barrier, 1, device_id=(s - G, e), device_id_type=MESH)

    @pl.when(g < NG - 1)
    def _():
        pl.semaphore_signal(barrier, 1, device_id=(s + G, e), device_id_type=MESH)

    wr = features // W_COPIES
    w_copies = [
        pltpu.make_async_copy(
            w_hbm.at[pl.ds(i * wr, wr)], w_ref.at[pl.ds(i * wr, wr)], w_sem.at[i]
        )
        for i in range(W_COPIES)
    ]

    ld = ld_ref[...]
    rows = lax.broadcasted_iota(jnp.int32, (T, T), 0)
    cols = lax.broadcasted_iota(jnp.int32, (T, T), 1)
    lower = cols <= rows
    tril = jnp.where(lower, 1.0, 0.0).astype(F32)
    cum = jnp.dot(tril, ld, precision=lax.Precision.HIGHEST, preferred_element_type=F32)
    cum_row = lax.dot_general(
        ld, tril, (((0,), (1,)), ((), ())),
        precision=lax.Precision.HIGHEST, preferred_element_type=F32,
    )
    total_row = cum[T - 1 : T, :]
    key_w = jnp.exp(total_row - cum)
    grow = jnp.exp(cum)
    block_decay = jnp.broadcast_to(jnp.exp(cum_row[:, T - 1 : T]), (heads, HD))
    pad = dec_own.shape[1]
    for j in range(G):
        part = block_decay[j * HS : (j + 1) * HS, :]
        if pad > HS:
            part = jnp.concatenate([part, jnp.zeros((pad - HS, HD), F32)], axis=0)
        dec_own[j] = part

    def dec_copy(to, frm):
        return pltpu.make_async_remote_copy(
            src_ref=dec_own.at[to], dst_ref=dec_in.at[frm],
            send_sem=dec_s.at[to], recv_sem=dec_r.at[frm],
            device_id=(g * G + to, e), device_id_type=MESH,
        )

    def mem_copy(to, frm, u):
        return pltpu.make_async_remote_copy(
            src_ref=mem_own.at[to, u], dst_ref=mem_in.at[frm, u],
            send_sem=mem_s.at[to, u], recv_sem=mem_r.at[frm, u],
            device_id=(g * G + to, e), device_id_type=MESH,
        )

    def pre_copy(to, frm, u):
        return pltpu.make_async_remote_copy(
            src_ref=pre_out.at[to, u], dst_ref=pre_in.at[frm, u],
            send_sem=pre_s.at[to, u], recv_sem=pre_r.at[frm, u],
            device_id=(g * G + to, e), device_id_type=MESH,
        )

    def chain_copy(u):
        return pltpu.make_async_remote_copy(
            src_ref=chain_out.at[u], dst_ref=chain_in.at[u],
            send_sem=ch_s.at[u], recv_sem=ch_r.at[u],
            device_id=((s + G) % n, e), device_id_type=MESH,
        )

    for u in range(SUB):
        for j in range(G):
            for r in range(hb):
                h = j * HS + u * hb + r
                lanes = slice(h * HD, (h + 1) * HD)
                high, low = split_high_low(k_ref[:, lanes].astype(F32) * key_w[:, h : h + 1])
                value = v_ref[:, lanes]
                mem_own[j, u, r] = lax.dot_general(
                    jnp.concatenate([high, low], axis=0),
                    jnp.concatenate([value, value], axis=0),
                    (((0,), (0,)), ((), ())),
                    preferred_element_type=F32,
                )
        if u == 0:
            beside = (g + NG - 1) // NG + (2 * NG - 2 - g) // NG
            pl.semaphore_wait(barrier, (G - 1) + (nh - 1) + beside)
            for o in range(1, G):
                dec_copy(member(o), c).start()
        for o in range(1, G):
            mem_copy(member(o), c, u).start()
        mem_in[c, u] = mem_own[c, u]
    dec_in[c] = dec_own[c]
    for copy in w_copies:
        copy.start()

    for h in range(heads):
        lanes = slice(h * HD, (h + 1) * HD)
        scores = lax.dot_general(
            q_ref[:, lanes], k_ref[:, lanes], (((1,), (1,)), ((), ())),
            preferred_element_type=F32,
        )
        diffs = jnp.where(lower, cum[:, h : h + 1] - cum_row[h : h + 1, :], 0.0)
        weights = (jnp.where(lower, jnp.exp(diffs), 0.0) * scores).astype(BF16)
        intra[h] = jnp.dot(weights, v_ref[:, lanes], preferred_element_type=F32)
        ecb[h] = jnp.broadcast_to(grow[:, h : h + 1], (T, HD))
    nsteer = tab_ref.shape[0]
    ids = jnp.broadcast_to(ids_ref[...], (nsteer, T))
    onehot = jnp.where(ids == lax.broadcasted_iota(jnp.int32, (nsteer, T), 0), 1.0, 0.0).astype(BF16)
    acc[...] = jnp.zeros_like(acc)
    acc[:, pl.ds(pl.multiple_of(e * CW, CW), CW)] = lax.dot_general(
        onehot, tab_ref[...], (((0,), (0,)), ((), ())), preferred_element_type=F32
    )

    for o in range(1, G):
        dec_copy(c, member(o)).wait_recv()
    for u in range(SUB):
        for o in range(1, G):
            mem_copy(c, member(o), u).wait_recv()

        @pl.when(g > 0)
        def _():
            chain_copy(u).wait_recv()

        @pl.when(g == 0)
        def _():
            chain_in[u] = jnp.zeros(chain_in.shape[1:], F32)

        for r in range(hb):
            state = chain_in[u, r]
            row = u * hb + r
            for j in range(G):
                pre_out[j, u, r] = state
                state = state * dec_in[j, row : row + 1, :] + mem_in[j, u, r]
            chain_out[u, r] = state

        @pl.when(g < NG - 1)
        def _():
            chain_copy(u).start()

        for o in range(1, G):
            pre_copy(member(o), c, u).start()
        pre_in[c, u] = pre_out[c, u]

    def normed_chunk(j, u):
        parts = []
        for r in range(hb):
            h = j * HS + u * hb + r
            lanes = pl.ds(pl.multiple_of(h * HD, HD), HD)
            high, low = split_high_low(pre_in[j, u, r])
            query = q_ref[:, lanes]
            carried = jnp.dot(
                jnp.concatenate([query, query], axis=1),
                jnp.concatenate([high, low], axis=0),
                preferred_element_type=F32,
            )
            attended = intra[h] + ecb[h] * carried
            mean_sq = jnp.mean(attended * attended, axis=1, keepdims=True)
            normed = attended * lax.rsqrt(mean_sq + 1e-6) * gain_ref[:, lanes]
            parts.append(normed.astype(BF16))
        return parts[0] if hb == 1 else jnp.concatenate(parts, axis=1)

    def w_rows(j, u):
        return pl.ds(pl.multiple_of((j * HS + u * hb) * HD, HD), hb * HD)

    for copy in w_copies:
        copy.wait()

    def step(i, carry):
        u, o = i // G, i % G
        j = (c + o) % G

        @pl.when(o > 0)
        def _():
            pre_copy(c, j, u).wait_recv()

        chunk = normed_chunk(j, u)
        for t in range(width // TW):
            at = slice(t * TW, (t + 1) * TW)
            acc[:, at] += jnp.dot(chunk, w_ref[w_rows(j, u), at], preferred_element_type=F32)
        return carry

    lax.fori_loop(0, G * SUB - 1, step, 0)

    last = (c + G - 1) % G
    pre_copy(c, last, SUB - 1).wait_recv()
    chunk = normed_chunk(last, SUB - 1)
    rows_last = w_rows(last, SUB - 1)

    def x_copy(o, t):
        return pltpu.make_async_remote_copy(
            src_ref=xout.at[o - 1, t], dst_ref=xin.at[o - 1, t],
            send_sem=x_s.at[o - 1, t], recv_sem=x_r.at[o - 1, t],
            device_id=(s, (e + o) % nh), device_id_type=MESH,
        )

    for o in range(1, nh):
        to = (e + o) % nh
        for t in range(nt):
            at = pl.ds(pl.multiple_of(to * CW + t * TW, TW), TW)
            xout[o - 1, t] = acc[:, at] + jnp.dot(
                chunk, w_ref[rows_last, at], preferred_element_type=F32
            )
            x_copy(o, t).start()
    for t in range(nt):
        at = pl.ds(pl.multiple_of(e * CW + t * TW, TW), TW)
        acc[:, at] += jnp.dot(chunk, w_ref[rows_last, at], preferred_element_type=F32)
    for t in range(nt):
        at = pl.ds(pl.multiple_of(e * CW + t * TW, TW), TW)
        whole = acc[:, at]
        for o in range(1, nh):
            x_copy(o, t).wait_recv()
            whole = whole + xin[o - 1, t]
        out_ref[:, t * TW : (t + 1) * TW] = whole.astype(BF16)

    for o in range(1, G):
        dec_copy(member(o), c).wait_send()
        for u in range(SUB):
            mem_copy(member(o), c, u).wait_send()
            pre_copy(member(o), c, u).wait_send()
    for o in range(1, nh):
        for t in range(nt):
            x_copy(o, t).wait_send()

    @pl.when(g < NG - 1)
    def _():
        for u in range(SUB):
            chain_copy(u).wait_send()


def solution(mesh):
    n, nh = mesh.shape["seq"], mesh.shape["head"]

    def shards(queries, keys, values, log_decay, norm_gain, out_weight, steer_ids, steer_table):
        T, features = queries.shape
        heads = log_decay.shape[1]
        HD = features // heads
        width = out_weight.shape[1]
        CW = width // nh
        G = 4
        HS = heads // G
        hb = 2 if HS % 2 == 0 else 1
        SUB = HS // hb
        nt = max(1, CW // 512)
        TW = CW // nt
        pad = (HS + 7) // 8 * 8
        DMA = pltpu.SemaphoreType.DMA
        vmem = pl.BlockSpec(memory_space=pltpu.VMEM)
        return pl.pallas_call(
            functools.partial(kernel, n, nh, G, SUB, hb, nt),
            out_shape=jax.ShapeDtypeStruct((T, CW), BF16),
            in_specs=[vmem] * 5 + [pl.BlockSpec(memory_space=pl.ANY)] + [vmem] * 2,
            out_specs=vmem,
            scratch_shapes=[
                pltpu.VMEM((features, width), BF16),
                pltpu.VMEM((G, SUB, hb, HD, HD), F32),
                pltpu.VMEM((G, pad, HD), F32),
                pltpu.VMEM((G, SUB, hb, HD, HD), F32),
                pltpu.VMEM((G, pad, HD), F32),
                pltpu.VMEM((SUB, hb, HD, HD), F32),
                pltpu.VMEM((SUB, hb, HD, HD), F32),
                pltpu.VMEM((G, SUB, hb, HD, HD), F32),
                pltpu.VMEM((G, SUB, hb, HD, HD), F32),
                pltpu.VMEM((heads, T, HD), F32),
                pltpu.VMEM((heads, T, HD), F32),
                pltpu.VMEM((T, width), F32),
                pltpu.VMEM((nh - 1, nt, T, TW), F32),
                pltpu.VMEM((nh - 1, nt, T, TW), F32),
                DMA((W_COPIES,)),
                DMA((G, SUB)), DMA((G, SUB)),
                DMA((G,)), DMA((G,)),
                DMA((SUB,)), DMA((SUB,)),
                DMA((G, SUB)), DMA((G, SUB)),
                DMA((nh - 1, nt)), DMA((nh - 1, nt)),
            ],
            compiler_params=pltpu.CompilerParams(
                collective_id=0, has_side_effects=True, vmem_limit_bytes=52 * 1024 * 1024
            ),
            cost_estimate=pl.CostEstimate(
                flops=2 * T * features * width,
                bytes_accessed=2 * features * width,
                transcendentals=T * T * heads,
            ),
        )(
            queries, keys, values, log_decay, norm_gain.reshape(1, features), out_weight,
            steer_ids.reshape(1, T), steer_table,
        )

    in_specs = (
        P("seq", "head"), P("seq", "head"), P("seq", "head"), P("seq", "head"),
        P("head"), P("head", None), P("seq"), P(None, "head"),
    )
    return jax.shard_map(
        shards, mesh=mesh, in_specs=in_specs, out_specs=P("seq", "head"), check_vma=False
    )
```

time: 272 us -> 46.7 us (0.17)
  the two profiles are of different devices: /device:TPU:25 before, /device:TPU:31 now
where the time goes in v1:
time: 46.7 us; the launch traced here: 46.3 us
  Pallas kernels  40.4 us (87%)
  local copies, waits for them, and re-layouts  5.86 us (13%)
    pallas_call x1, Pallas kernels, shards(): pl.pallas_call(functools.partial(kernel, n, nh, G, SUB, hb, nt), out_shap...  40.4 us
    unnamed x12, local copies, waits for them, and re-layouts  5.86 us

profile of v1, /device:TPU:31, one launch (start us, length us, event | category | flops | bytes accessed | tf_op | source)
XLA Modules:
  0.0 46.3 jit_solution(6278851576218635858)
XLA Ops:
  0.0 0.8 %copy.9.ld_ref = f32[128,16]{1,0:T(8,128)S(1)} copy(f32[128,16]{0,1:T(8,128)} %param.11) | data formatting | bytes 16384 | tf_op args[3]
  0.8 0.0 copy-start
  0.8 1.0 %copy-done = bf16[128,2048]{1,0:T(8,128)(2,1)S(1)} copy-done((bf16[128,2048]{1,0:T(8,128)(2,1)S(1)}, bf16[128,2048]{1,0:T(8,128)(2,1)}, u32[]{:S(2)}) %copy-start) | copy-done | bytes 524312
  1.8 0.0 copy-start.1
  1.8 1.0 %copy-done.1 = bf16[128,2048]{1,0:T(8,128)(2,1)S(1)} copy-done((bf16[128,2048]{1,0:T(8,128)(2,1)S(1)}, bf16[128,2048]{1,0:T(8,128)(2,1)}, u32[]{:S(2)}) %copy-start.1) | copy-done | bytes 524312
  2.9 0.0 copy-start.2
  2.9 0.8 %copy-done.2 = bf16[16,2048]{1,0:T(8,128)(2,1)S(1)} copy-done((bf16[16,2048]{1,0:T(8,128)(2,1)S(1)}, bf16[16,2048]{1,0:T(8,128)(2,1)}, u32[]{:S(2)}) %copy-start.2) | copy-done | bytes 65560
  3.7 0.0 copy-start.3
  3.7 0.7 %copy-done.3 = f32[2048]{0:T(1024)S(1)} copy-done((f32[2048]{0:T(1024)S(1)}, f32[2048]{0:T(1024)}, u32[]{:S(2)}) %copy-start.3) | copy-done | bytes 8216
  4.4 0.0 copy-start.4
  4.4 0.7 %copy-done.4 = s32[128]{0:T(128)S(1)} copy-done((s32[128]{0:T(128)S(1)}, s32[128]{0:T(128)}, u32[]{:S(2)}) %copy-start.4) | copy-done | bytes 536
  5.1 40.4 %shard_map.82 = bf16[128,2048]{1,0:T(8,128)(2,1)S(1)} custom-call(bf16[128,2048]{1,0:T(8,128)(2,1)S(1)} %copy-done, bf16[128,2048]{1,0:T(8,128)(2,1)S(1)} %copy-done.1, bf16[128,2048]{1,0:T(8,128)(2,1)} %v_ref.1, f32[128,16]{1,0:T(8,128)S(1)} %copy.9.ld_ref, f32[1,2048]{1,0:T(1,128)S(1)} %bitcast.2, bf16[2048,4096]{1,0:T(8,128)(2,1)} %w_hbm.1, ...), custom_call_target="tpu_custom_call" | custom-call | flops 2147483648 | bytes 16777216 | tf_op jit(solution)/shard_map/pallas_call | solution.py:293
  45.5 0.8 %copy.11 = bf16[128,2048]{1,0:T(8,128)(2,1)} copy(bf16[128,2048]{1,0:T(8,128)(2,1)S(1)} %shard_map.82) | data formatting | bytes 1048576
Async XLA Ops:
  0.8 1.0 %copy-start = (bf16[128,2048]{1,0:T(8,128)(2,1)S(1)}, bf16[128,2048]{1,0:T(8,128)(2,1)}, u32[]{:S(2)}) copy-start(bf16[128,2048]{1,0:T(8,128)(2,1)} %q_ref.1) | copy-start | bytes 1572868
  1.8 1.0 %copy-start.1 = (bf16[128,2048]{1,0:T(8,128)(2,1)S(1)}, bf16[128,2048]{1,0:T(8,128)(2,1)}, u32[]{:S(2)}) copy-start(bf16[128,2048]{1,0:T(8,128)(2,1)} %k_ref.1) | copy-start | bytes 1572868
  2.9 0.8 %copy-start.2 = (bf16[16,2048]{1,0:T(8,128)(2,1)S(1)}, bf16[16,2048]{1,0:T(8,128)(2,1)}, u32[]{:S(2)}) copy-start(bf16[16,2048]{1,0:T(8,128)(2,1)} %tab_ref.1) | copy-start | bytes 196612
  3.7 0.7 %copy-start.3 = (f32[2048]{0:T(1024)S(1)}, f32[2048]{0:T(1024)}, u32[]{:S(2)}) copy-start(f32[2048]{0:T(1024)} %param.12) | copy-start | bytes 24580
  4.4 0.7 %copy-start.4 = (s32[128]{0:T(128)S(1)}, s32[128]{0:T(128)}, u32[]{:S(2)}) copy-start(s32[128]{0:T(128)} %param.14) | copy-start | bytes 1540

commit v2 on v1

--- a/solution.py
+++ b/solution.py
@@ -20,13 +20,14 @@
 
 def kernel(
     n, nh, G, SUB, hb, nt,
-    q_ref, k_ref, v_ref, ld_ref, gain_ref, w_hbm, ids_ref, tab_ref,
+    q_hbm, k_hbm, v_hbm, ld_hbm, gain_hbm, w_hbm, ids_hbm, tab_hbm,
     out_ref,
+    q_ref, k_ref, v_ref, ld_ref, gain_ref, ids_ref, tab_ref, in_sem,
     w_ref, mem_own, dec_own, mem_in, dec_in, chain_out, chain_in, pre_out, pre_in,
     intra, ecb, acc, xout, xin,
     w_sem, mem_s, mem_r, dec_s, dec_r, ch_s, ch_r, pre_s, pre_r, x_s, x_r,
 ):
-    T, features = q_ref.shape
+    T, features = q_hbm.shape
     HD = 128
     heads = features // HD
     HS = heads // G
@@ -39,8 +40,24 @@
     g = s // G
     c = s % G
 
-    def member(o):
-        return (c + o) % G
+    def member(i):
+        o, bit, rank = (G - i) % G, 1, 0
+        while bit < G:
+            rank = rank + (c // bit + o // bit) % 2 * bit
+            bit *= 2
+        return rank
+
+    fetch_ld, fetch_k, fetch_v, fetch_q, fetch_gain, fetch_ids, fetch_tab = [
+        pltpu.make_async_copy(src, dst, in_sem.at[i])
+        for i, (src, dst) in enumerate(
+            [
+                (ld_hbm, ld_ref), (k_hbm, k_ref), (v_hbm, v_ref), (q_hbm, q_ref),
+                (gain_hbm, gain_ref), (ids_hbm, ids_ref), (tab_hbm, tab_ref),
+            ]
+        )
+    ]
+    for copy in (fetch_ld, fetch_k, fetch_v, fetch_q, fetch_gain, fetch_ids, fetch_tab):
+        copy.start()
 
     barrier = pltpu.get_barrier_semaphore()
     for o in range(1, G):
@@ -64,14 +81,18 @@
         for i in range(W_COPIES)
     ]
 
+    fetch_ld.wait()
     ld = ld_ref[...]
     rows = lax.broadcasted_iota(jnp.int32, (T, T), 0)
     cols = lax.broadcasted_iota(jnp.int32, (T, T), 1)
     lower = cols <= rows
     tril = jnp.where(lower, 1.0, 0.0).astype(F32)
-    cum = jnp.dot(tril, ld, precision=lax.Precision.HIGHEST, preferred_element_type=F32)
+    cum = lax.dot_general(
+        tril, ld, (((1,), (1,)), ((), ())),
+        precision=lax.Precision.HIGHEST, preferred_element_type=F32,
+    )
     cum_row = lax.dot_general(
-        ld, tril, (((0,), (1,)), ((), ())),
+        ld, tril, (((1,), (1,)), ((), ())),
         precision=lax.Precision.HIGHEST, preferred_element_type=F32,
     )
     total_row = cum[T - 1 : T, :]
@@ -113,6 +134,8 @@
             device_id=((s + G) % n, e), device_id_type=MESH,
         )
 
+    fetch_k.wait()
+    fetch_v.wait()
     for u in range(SUB):
         for j in range(G):
             for r in range(hb):
@@ -138,6 +161,8 @@
     for copy in w_copies:
         copy.start()
 
+    for copy in (fetch_q, fetch_gain, fetch_ids, fetch_tab):
+        copy.wait()
     for h in range(heads):
         lanes = slice(h * HD, (h + 1) * HD)
         scores = lax.dot_general(
@@ -212,7 +237,7 @@
 
     def step(i, carry):
         u, o = i // G, i % G
-        j = (c + o) % G
+        j = member(o)
 
         @pl.when(o > 0)
         def _():
@@ -226,7 +251,7 @@
 
     lax.fori_loop(0, G * SUB - 1, step, 0)
 
-    last = (c + G - 1) % G
+    last = member(G - 1)
     pre_copy(c, last, SUB - 1).wait_recv()
     chunk = normed_chunk(last, SUB - 1)
     rows_last = w_rows(last, SUB - 1)
@@ -281,21 +306,28 @@
         HD = features // heads
         width = out_weight.shape[1]
         CW = width // nh
-        G = 4
+        G = 8 if heads % 8 == 0 else 4
         HS = heads // G
-        hb = 2 if HS % 2 == 0 else 1
+        hb = 1
         SUB = HS // hb
         nt = max(1, CW // 512)
         TW = CW // nt
         pad = (HS + 7) // 8 * 8
         DMA = pltpu.SemaphoreType.DMA
-        vmem = pl.BlockSpec(memory_space=pltpu.VMEM)
         return pl.pallas_call(
             functools.partial(kernel, n, nh, G, SUB, hb, nt),
             out_shape=jax.ShapeDtypeStruct((T, CW), BF16),
-            in_specs=[vmem] * 5 + [pl.BlockSpec(memory_space=pl.ANY)] + [vmem] * 2,
-            out_specs=vmem,
+            in_specs=[pl.BlockSpec(memory_space=pltpu.HBM)] * 8,
+            out_specs=pl.BlockSpec(memory_space=pltpu.VMEM),
             scratch_shapes=[
+                pltpu.VMEM((T, features), BF16),
+                pltpu.VMEM((T, features), BF16),
+                pltpu.VMEM((T, features), BF16),
+                pltpu.VMEM((heads, T), F32),
+                pltpu.VMEM((1, features), F32),
+                pltpu.VMEM((1, T), jnp.int32),
+                pltpu.VMEM(steer_table.shape, BF16),
+                DMA((7,)),
                 pltpu.VMEM((features, width), BF16),
                 pltpu.VMEM((G, SUB, hb, HD, HD), F32),
                 pltpu.VMEM((G, pad, HD), F32),
@@ -326,7 +358,7 @@
                 transcendentals=T * T * heads,
             ),
         )(
-            queries, keys, values, log_decay, norm_gain.reshape(1, features), out_weight,
+            queries, keys, values, log_decay.T, norm_gain.reshape(1, features), out_weight,
             steer_ids.reshape(1, T), steer_table,
         )
 

time: 46.7 us -> 46.3 us (level)
  the two profiles are of different devices: /device:TPU:31 before, /device:TPU:21 now
where the time goes in v2:
time: 46.3 us; the launch traced here: 45.9 us
  Pallas kernels  40.1 us (87%)
  local copies, waits for them, and re-layouts  5.76 us (12%)
    pallas_call x1, Pallas kernels, shards(): pl.pallas_call(functools.partial(kernel, n, nh, G, SUB, hb, nt), out_shap...  40.1 us
    unnamed x13, local copies, waits for them, and re-layouts  5.76 us

profile of v2, /device:TPU:21, one launch (start us, length us, event | category | flops | bytes accessed | tf_op | source)
XLA Modules:
  0.0 45.9 jit_solution(13631653906311413946)
XLA Ops:
  0.0 0.0 copy-start
  0.0 1.0 %copy-done = bf16[128,2048]{1,0:T(8,128)(2,1)S(1)} copy-done((bf16[128,2048]{1,0:T(8,128)(2,1)S(1)}, bf16[128,2048]{1,0:T(8,128)(2,1)}, u32[]{:S(2)}) %copy-start) | copy-done | bytes 524312
  1.0 0.0 copy-start.1
  1.0 1.0 %copy-done.1 = bf16[128,2048]{1,0:T(8,128)(2,1)S(1)} copy-done((bf16[128,2048]{1,0:T(8,128)(2,1)S(1)}, bf16[128,2048]{1,0:T(8,128)(2,1)}, u32[]{:S(2)}) %copy-start.1) | copy-done | bytes 524312
  2.1 0.0 copy-start.2
  2.1 0.8 %copy-done.2 = bf16[16,2048]{1,0:T(8,128)(2,1)S(1)} copy-done((bf16[16,2048]{1,0:T(8,128)(2,1)S(1)}, bf16[16,2048]{1,0:T(8,128)(2,1)}, u32[]{:S(2)}) %copy-start.2) | copy-done | bytes 65560
  2.9 0.0 copy-start.3
  2.9 0.7 %copy-done.3 = f32[128,16]{0,1:T(8,128)S(1)} copy-done((f32[128,16]{0,1:T(8,128)S(1)}, f32[128,16]{0,1:T(8,128)}, u32[]{:S(2)}) %copy-start.3) | copy-done | bytes 8216
  3.6 0.0 copy-start.4
  3.6 0.7 %copy-done.4 = f32[2048]{0:T(1024)S(1)} copy-done((f32[2048]{0:T(1024)S(1)}, f32[2048]{0:T(1024)}, u32[]{:S(2)}) %copy-start.4) | copy-done | bytes 8216
  4.3 0.0 copy-start.5
  4.3 0.7 %copy-done.5 = s32[128]{0:T(128)S(1)} copy-done((s32[128]{0:T(128)S(1)}, s32[128]{0:T(128)}, u32[]{:S(2)}) %copy-start.5) | copy-done | bytes 536
  5.0 40.1 %shard_map.82 = bf16[128,2048]{1,0:T(8,128)(2,1)S(1)} custom-call(bf16[128,2048]{1,0:T(8,128)(2,1)S(1)} %copy-done, bf16[128,2048]{1,0:T(8,128)(2,1)S(1)} %copy-done.1, bf16[128,2048]{1,0:T(8,128)(2,1)} %v_hbm.1, f32[16,128]{1,0:T(8,128)S(1)} %bitcast.3, f32[1,2048]{1,0:T(1,128)S(1)} %bitcast.4, bf16[2048,4096]{1,0:T(8,128)(2,1)} %w_hbm.1, ...), custom_call_target="tpu_custom_call" | custom-call | flops 2147483648 | bytes 16777216 | tf_op jit(solution)/shard_map/pallas_call | solution.py:317
  45.1 0.8 %copy.10 = bf16[128,2048]{1,0:T(8,128)(2,1)} copy(bf16[128,2048]{1,0:T(8,128)(2,1)S(1)} %shard_map.82) | data formatting | bytes 1048576
Async XLA Ops:
  0.0 1.0 %copy-start = (bf16[128,2048]{1,0:T(8,128)(2,1)S(1)}, bf16[128,2048]{1,0:T(8,128)(2,1)}, u32[]{:S(2)}) copy-start(bf16[128,2048]{1,0:T(8,128)(2,1)} %q_hbm.1) | copy-start | bytes 1572868
  1.0 1.0 %copy-start.1 = (bf16[128,2048]{1,0:T(8,128)(2,1)S(1)}, bf16[128,2048]{1,0:T(8,128)(2,1)}, u32[]{:S(2)}) copy-start(bf16[128,2048]{1,0:T(8,128)(2,1)} %k_hbm.1) | copy-start | bytes 1572868
  2.1 0.8 %copy-start.2 = (bf16[16,2048]{1,0:T(8,128)(2,1)S(1)}, bf16[16,2048]{1,0:T(8,128)(2,1)}, u32[]{:S(2)}) copy-start(bf16[16,2048]{1,0:T(8,128)(2,1)} %tab_hbm.1) | copy-start | bytes 196612
  2.9 0.7 %copy-start.3 = (f32[128,16]{0,1:T(8,128)S(1)}, f32[128,16]{0,1:T(8,128)}, u32[]{:S(2)}) copy-start(f32[128,16]{0,1:T(8,128)} %param.11) | copy-start | bytes 24580
  3.6 0.7 %copy-start.4 = (f32[2048]{0:T(1024)S(1)}, f32[2048]{0:T(1024)}, u32[]{:S(2)}) copy-start(f32[2048]{0:T(1024)} %param.12) | copy-start | bytes 24580
  4.3 0.7 %copy-start.5 = (s32[128]{0:T(128)S(1)}, s32[128]{0:T(128)}, u32[]{:S(2)}) copy-start(s32[128]{0:T(128)} %param.14) | copy-start | bytes 1540

commit v3 on v2

--- a/solution.py
+++ b/solution.py
@@ -136,27 +136,33 @@
 
     fetch_k.wait()
     fetch_v.wait()
+    for h in range(heads):
+        intra[h] = jnp.broadcast_to(key_w[:, h : h + 1], (T, HD))
     for u in range(SUB):
-        for j in range(G):
+        for i in list(range(1, G)) + [0]:
+            to = member(i)
             for r in range(hb):
-                h = j * HS + u * hb + r
-                lanes = slice(h * HD, (h + 1) * HD)
-                high, low = split_high_low(k_ref[:, lanes].astype(F32) * key_w[:, h : h + 1])
+                h = to * HS + u * hb + r
+                lanes = pl.ds(pl.multiple_of(h * HD, HD), HD)
+                high, low = split_high_low(k_ref[:, lanes].astype(F32) * intra[h])
                 value = v_ref[:, lanes]
-                mem_own[j, u, r] = lax.dot_general(
+                memory = lax.dot_general(
                     jnp.concatenate([high, low], axis=0),
                     jnp.concatenate([value, value], axis=0),
                     (((0,), (0,)), ((), ())),
                     preferred_element_type=F32,
                 )
-        if u == 0:
-            beside = (g + NG - 1) // NG + (2 * NG - 2 - g) // NG
-            pl.semaphore_wait(barrier, (G - 1) + (nh - 1) + beside)
-            for o in range(1, G):
-                dec_copy(member(o), c).start()
-        for o in range(1, G):
-            mem_copy(member(o), c, u).start()
-        mem_in[c, u] = mem_own[c, u]
+                if i == 0:
+                    mem_in[c, u, r] = memory
+                else:
+                    mem_own[to, u, r] = memory
+            if u == 0 and i == 1:
+                beside = (g + NG - 1) // NG + (2 * NG - 2 - g) // NG
+                pl.semaphore_wait(barrier, (G - 1) + (nh - 1) + beside)
+                for o in range(1, G):
+                    dec_copy(member(o), c).start()
+            if i > 0:
+                mem_copy(to, c, u).start()
     dec_in[c] = dec_own[c]
     for copy in w_copies:
         copy.start()
@@ -211,50 +217,58 @@
             pre_copy(member(o), c, u).start()
         pre_in[c, u] = pre_out[c, u]
 
-    def normed_chunk(j, u):
+    pair = 2 if SUB % 2 == 0 else 1
+
+    def normed_chunk(j, p):
         parts = []
-        for r in range(hb):
-            h = j * HS + u * hb + r
-            lanes = pl.ds(pl.multiple_of(h * HD, HD), HD)
-            high, low = split_high_low(pre_in[j, u, r])
-            query = q_ref[:, lanes]
-            carried = jnp.dot(
-                jnp.concatenate([query, query], axis=1),
-                jnp.concatenate([high, low], axis=0),
-                preferred_element_type=F32,
-            )
-            attended = intra[h] + ecb[h] * carried
-            mean_sq = jnp.mean(attended * attended, axis=1, keepdims=True)
-            normed = attended * lax.rsqrt(mean_sq + 1e-6) * gain_ref[:, lanes]
-            parts.append(normed.astype(BF16))
-        return parts[0] if hb == 1 else jnp.concatenate(parts, axis=1)
-
-    def w_rows(j, u):
-        return pl.ds(pl.multiple_of((j * HS + u * hb) * HD, HD), hb * HD)
+        for d in range(pair):
+            u = p * pair + d
+            for r in range(hb):
+                h = j * HS + u * hb + r
+                lanes = pl.ds(pl.multiple_of(h * HD, HD), HD)
+                high, low = split_high_low(pre_in[j, u, r])
+                query = q_ref[:, lanes]
+                carried = jnp.dot(
+                    jnp.concatenate([query, query], axis=1),
+                    jnp.concatenate([high, low], axis=0),
+                    preferred_element_type=F32,
+                )
+                attended = intra[h] + ecb[h] * carried
+                mean_sq = jnp.mean(attended * attended, axis=1, keepdims=True)
+                normed = attended * lax.rsqrt(mean_sq + 1e-6) * gain_ref[:, lanes]
+                parts.append(normed.astype(BF16))
+        return parts[0] if len(parts) == 1 else jnp.concatenate(parts, axis=1)
+
+    def w_rows(j, p):
+        depth = pair * hb * HD
+        return pl.ds(pl.multiple_of(j * HS * HD + p * depth, HD), depth)
 
     for copy in w_copies:
         copy.wait()
 
     def step(i, carry):
-        u, o = i // G, i % G
+        p, o = i // G, i % G
         j = member(o)
 
         @pl.when(o > 0)
         def _():
-            pre_copy(c, j, u).wait_recv()
-
-        chunk = normed_chunk(j, u)
+            for d in range(pair):
+                pre_copy(c, j, p * pair + d).wait_recv()
+
+        chunk = normed_chunk(j, p)
         for t in range(width // TW):
             at = slice(t * TW, (t + 1) * TW)
-            acc[:, at] += jnp.dot(chunk, w_ref[w_rows(j, u), at], preferred_element_type=F32)
+            acc[:, at] += jnp.dot(chunk, w_ref[w_rows(j, p), at], preferred_element_type=F32)
         return carry
 
-    lax.fori_loop(0, G * SUB - 1, step, 0)
+    lax.fori_loop(0, G * (SUB // pair) - 1, step, 0)
 
     last = member(G - 1)
-    pre_copy(c, last, SUB - 1).wait_recv()
-    chunk = normed_chunk(last, SUB - 1)
-    rows_last = w_rows(last, SUB - 1)
+    final = SUB // pair - 1
+    for d in range(pair):
+        pre_copy(c, last, final * pair + d).wait_recv()
+    chunk = normed_chunk(last, final)
+    rows_last = w_rows(last, final)
 
     def x_copy(o, t):
         return pltpu.make_async_remote_copy(
@@ -306,7 +320,7 @@
         HD = features // heads
         width = out_weight.shape[1]
         CW = width // nh
-        G = 8 if heads % 8 == 0 else 4
+        G = 4
         HS = heads // G
         hb = 1
         SUB = HS // hb
@@ -350,7 +364,7 @@
                 DMA((nh - 1, nt)), DMA((nh - 1, nt)),
             ],
             compiler_params=pltpu.CompilerParams(
-                collective_id=0, has_side_effects=True, vmem_limit_bytes=52 * 1024 * 1024
+                collective_id=0, has_side_effects=True, vmem_limit_bytes=60 * 1024 * 1024
             ),
             cost_estimate=pl.CostEstimate(
                 flops=2 * T * features * width,

time: 46.3 us -> 37.2 us (0.80)
  the two profiles are of different devices: /device:TPU:21 before, /device:TPU:25 now
where the time goes in v3:
time: 37.2 us; the launch traced here: 37 us
  Pallas kernels  35.1 us (94%)
  local copies, waits for them, and re-layouts  1.88 us (5%)
    pallas_call x1, Pallas kernels, shards(): pl.pallas_call(functools.partial(kernel, n, nh, G, SUB, hb, nt), out_shap...  35.1 us
    unnamed x1, local copies, waits for them, and re-layouts  1.88 us

profile of v3, /device:TPU:25, one launch (start us, length us, event | category | flops | bytes accessed | tf_op | source)
XLA Modules:
  0.0 37.0 jit_solution(5448031242354090990)
XLA Ops:
  0.0 35.1 %shard_map.82 = bf16[128,2048]{1,0:T(8,128)(2,1)} custom-call(bf16[128,2048]{1,0:T(8,128)(2,1)} %q_hbm.1, bf16[128,2048]{1,0:T(8,128)(2,1)} %k_hbm.1, bf16[128,2048]{1,0:T(8,128)(2,1)} %v_hbm.1, f32[16,128]{1,0:T(8,128)} %bitcast.3, f32[1,2048]{1,0:T(1,128)} %bitcast.4, bf16[2048,4096]{1,0:T(8,128)(2,1)} %w_hbm.1, s32[1,128]{1,0:T(1,128)} %bitcast.5, ...), custom_call_target="tpu_custom_call" | custom-call | flops 2147483648 | bytes 16777216 | tf_op jit(solution)/shard_map/pallas_call | solution.py:331
  35.1 1.9 %copy.10 = bf16[128,2048]{1,0:T(8,128)(2,1)} copy(bf16[128,2048]{1,0:T(8,128)(2,1)} %shard_map.82) | data formatting | bytes 1048576

commit v4 on v3

--- a/solution.py
+++ b/solution.py
@@ -24,8 +24,8 @@
     out_ref,
     q_ref, k_ref, v_ref, ld_ref, gain_ref, ids_ref, tab_ref, in_sem,
     w_ref, mem_own, dec_own, mem_in, dec_in, chain_out, chain_in, pre_out, pre_in,
-    intra, ecb, acc, xout, xin,
-    w_sem, mem_s, mem_r, dec_s, dec_r, ch_s, ch_r, pre_s, pre_r, x_s, x_r,
+    intra, ecb, acc, xout, xin, late_w_out, late_w_in, late_out, late_in,
+    w_sem, mem_s, mem_r, dec_s, dec_r, ch_s, ch_r, pre_s, pre_r, x_s, x_r, lw_s, lw_r, la_s, la_r,
 ):
     T, features = q_hbm.shape
     HD = 128
@@ -261,40 +261,72 @@
             acc[:, at] += jnp.dot(chunk, w_ref[w_rows(j, p), at], preferred_element_type=F32)
         return carry
 
-    lax.fori_loop(0, G * (SUB // pair) - 1, step, 0)
-
     last = member(G - 1)
     final = SUB // pair - 1
+    rows_last = w_rows(last, final)
+
+    def late_w_copy(o):
+        return pltpu.make_async_remote_copy(
+            src_ref=late_w_out.at[o - 1], dst_ref=late_w_in.at[o - 1],
+            send_sem=lw_s.at[o - 1], recv_sem=lw_r.at[o - 1],
+            device_id=(s, (e + o) % nh), device_id_type=MESH,
+        )
+
+    def late_copy(o):
+        return pltpu.make_async_remote_copy(
+            src_ref=late_out, dst_ref=late_in.at[o - 1],
+            send_sem=la_s.at[o - 1], recv_sem=la_r.at[o - 1],
+            device_id=(s, (e + o) % nh), device_id_type=MESH,
+        )
+
+    def x_copy(o, t):
+        return pltpu.make_async_remote_copy(
+            src_ref=xout.at[o - 1, t], dst_ref=xin.at[o - 1, t],
+            send_sem=x_s.at[o - 1, t], recv_sem=x_r.at[o - 1, t],
+            device_id=(s, (e + o) % nh), device_id_type=MESH,
+        )
+
+    def columns(group, t):
+        return pl.ds(pl.multiple_of(group * CW + t * TW, TW), TW)
+
+    for o in range(1, nh):
+        to = (e + o) % nh
+        for t in range(nt):
+            late_w_out[o - 1, :, t * TW : (t + 1) * TW] = w_ref[rows_last, columns(to, t)].astype(F32)
+        late_w_copy(o).start()
+
+    lax.fori_loop(0, G * (SUB // pair) - 1, step, 0)
+
+    for o in range(1, nh):
+        to = (e + o) % nh
+        for t in range(nt):
+            xout[o - 1, t] = acc[:, columns(to, t)]
+            x_copy(o, t).start()
+
     for d in range(pair):
         pre_copy(c, last, final * pair + d).wait_recv()
     chunk = normed_chunk(last, final)
-    rows_last = w_rows(last, final)
-
-    def x_copy(o, t):
-        return pltpu.make_async_remote_copy(
-            src_ref=xout.at[o - 1, t], dst_ref=xin.at[o - 1, t],
-            send_sem=x_s.at[o - 1, t], recv_sem=x_r.at[o - 1, t],
-            device_id=(s, (e + o) % nh), device_id_type=MESH,
-        )
-
-    for o in range(1, nh):
-        to = (e + o) % nh
+    late_out[...] = chunk.astype(F32)
+    for o in range(1, nh):
+        late_copy(o).start()
+    for t in range(nt):
+        at = columns(e, t)
+        acc[:, at] += jnp.dot(chunk, w_ref[rows_last, at], preferred_element_type=F32)
+    for o in range(1, nh):
+        late_w_copy(o).wait_recv()
         for t in range(nt):
-            at = pl.ds(pl.multiple_of(to * CW + t * TW, TW), TW)
-            xout[o - 1, t] = acc[:, at] + jnp.dot(
-                chunk, w_ref[rows_last, at], preferred_element_type=F32
+            x_copy(o, t).wait_recv()
+    for o in range(1, nh):
+        late_copy(o).wait_recv()
+    for t in range(nt):
+        at = slice(t * TW, (t + 1) * TW)
+        whole = acc[:, columns(e, t)]
+        for o in range(1, nh):
+            whole = whole + xin[o - 1, t] + jnp.dot(
+                late_in[o - 1].astype(BF16), late_w_in[o - 1, :, at].astype(BF16),
+                preferred_element_type=F32,
             )
-            x_copy(o, t).start()
-    for t in range(nt):
-        at = pl.ds(pl.multiple_of(e * CW + t * TW, TW), TW)
-        acc[:, at] += jnp.dot(chunk, w_ref[rows_last, at], preferred_element_type=F32)
-    for t in range(nt):
-        at = pl.ds(pl.multiple_of(e * CW + t * TW, TW), TW)
-        whole = acc[:, at]
-        for o in range(1, nh):
-            x_copy(o, t).wait_recv()
-            whole = whole + xin[o - 1, t]
-        out_ref[:, t * TW : (t + 1) * TW] = whole.astype(BF16)
+        out_ref[:, at] = whole.astype(BF16)
 
     for o in range(1, G):
         dec_copy(member(o), c).wait_send()
@@ -304,6 +336,8 @@
     for o in range(1, nh):
         for t in range(nt):
             x_copy(o, t).wait_send()
+        late_w_copy(o).wait_send()
+        late_copy(o).wait_send()
 
     @pl.when(g < NG - 1)
     def _():
@@ -327,6 +361,7 @@
         nt = max(1, CW // 512)
         TW = CW // nt
         pad = (HS + 7) // 8 * 8
+        late = (2 if SUB % 2 == 0 else 1) * hb * HD
         DMA = pltpu.SemaphoreType.DMA
         return pl.pallas_call(
             functools.partial(kernel, n, nh, G, SUB, hb, nt),
@@ -356,12 +391,18 @@
                 pltpu.VMEM((T, width), F32),
                 pltpu.VMEM((nh - 1, nt, T, TW), F32),
                 pltpu.VMEM((nh - 1, nt, T, TW), F32),
+                pltpu.VMEM((nh - 1, late, CW), F32),
+                pltpu.VMEM((nh - 1, late, CW), F32),
+                pltpu.VMEM((T, late), F32),
+                pltpu.VMEM((nh - 1, T, late), F32),
                 DMA((W_COPIES,)),
                 DMA((G, SUB)), DMA((G, SUB)),
                 DMA((G,)), DMA((G,)),
                 DMA((SUB,)), DMA((SUB,)),
                 DMA((G, SUB)), DMA((G, SUB)),
                 DMA((nh - 1, nt)), DMA((nh - 1, nt)),
+                DMA((nh - 1,)), DMA((nh - 1,)),
+                DMA((nh - 1,)), DMA((nh - 1,)),
             ],
             compiler_params=pltpu.CompilerParams(
                 collective_id=0, has_side_effects=True, vmem_limit_bytes=60 * 1024 * 1024

time: 37.2 us -> 37.4 us (level)
  no operation moved by 1% of the time
where the time goes in v4:
time: 37.4 us; the launch traced here: 37.3 us
  Pallas kernels  35.4 us (95%)
  local copies, waits for them, and re-layouts  1.88 us (5%)
    pallas_call x1, Pallas kernels, shards(): pl.pallas_call(functools.partial(kernel, n, nh, G, SUB, hb, nt), out_shap...  35.4 us
    unnamed x1, local copies, waits for them, and re-layouts  1.88 us

profile of v4, /device:TPU:25, one launch (start us, length us, event | category | flops | bytes accessed | tf_op | source)
XLA Modules:
  0.0 37.3 jit_solution(1395843259352257033)
XLA Ops:
  0.0 35.4 %shard_map.82 = bf16[128,2048]{1,0:T(8,128)(2,1)} custom-call(bf16[128,2048]{1,0:T(8,128)(2,1)} %q_hbm.1, bf16[128,2048]{1,0:T(8,128)(2,1)} %k_hbm.1, bf16[128,2048]{1,0:T(8,128)(2,1)} %v_hbm.1, f32[16,128]{1,0:T(8,128)} %bitcast.3, f32[1,2048]{1,0:T(1,128)} %bitcast.4, bf16[2048,4096]{1,0:T(8,128)(2,1)} %w_hbm.1, s32[1,128]{1,0:T(1,128)} %bitcast.5, ...), custom_call_target="tpu_custom_call" | custom-call | flops 2147483648 | bytes 16777216 | tf_op jit(solution)/shard_map/pallas_call | solution.py:366
  35.4 1.9 %copy.10 = bf16[128,2048]{1,0:T(8,128)(2,1)} copy(bf16[128,2048]{1,0:T(8,128)(2,1)} %shard_map.82) | data formatting | bytes 1048576

commit v5 on v3

--- a/solution.py
+++ b/solution.py
@@ -161,7 +161,7 @@
                 pl.semaphore_wait(barrier, (G - 1) + (nh - 1) + beside)
                 for o in range(1, G):
                     dec_copy(member(o), c).start()
-            if i > 0:
+            if i > 0 and u < 2:
                 mem_copy(to, c, u).start()
     dec_in[c] = dec_own[c]
     for copy in w_copies:
@@ -170,6 +170,12 @@
     for copy in (fetch_q, fetch_gain, fetch_ids, fetch_tab):
         copy.wait()
     for h in range(heads):
+        if SUB > 2 and h % (heads // (SUB - 2)) == heads // (SUB - 2) - 1:
+            u = 2 + h // (heads // (SUB - 2))
+            for o in range(1, G):
+                mem_copy(member(o), c, u - 2).wait_send()
+            for o in range(1, G):
+                mem_copy(member(o), c, u).start()
         lanes = slice(h * HD, (h + 1) * HD)
         scores = lax.dot_general(
             q_ref[:, lanes], k_ref[:, lanes], (((1,), (1,)), ((), ())),
@@ -298,8 +304,9 @@
 
     for o in range(1, G):
         dec_copy(member(o), c).wait_send()
+        for u in range(max(0, SUB - 2), SUB):
+            mem_copy(member(o), c, u).wait_send()
         for u in range(SUB):
-            mem_copy(member(o), c, u).wait_send()
             pre_copy(member(o), c, u).wait_send()
     for o in range(1, nh):
         for t in range(nt):

time: 37.2 us -> 38.1 us (1.024)
  Pallas kernels: 35.1 us -> 36 us
    pallas_call x1, Pallas kernels: 35.1 us -> 36 us  [shards(): pl.pallas_call(functools.partial(kernel, n, nh, G, SUB, hb, nt), out_shap...]
where the time goes in v5:
time: 38.1 us; the launch traced here: 37.9 us
  Pallas kernels  36 us (94%)
  local copies, waits for them, and re-layouts  1.88 us (5%)
    pallas_call x1, Pallas kernels, shards(): pl.pallas_call(functools.partial(kernel, n, nh, G, SUB, hb, nt), out_shap...  36 us
    unnamed x1, local copies, waits for them, and re-layouts  1.88 us

profile of v5, /device:TPU:25, one launch (start us, length us, event | category | flops | bytes accessed | tf_op | source)
XLA Modules:
  0.0 37.9 jit_solution(2609581026513741595)
XLA Ops:
  0.0 36.0 %shard_map.82 = bf16[128,2048]{1,0:T(8,128)(2,1)} custom-call(bf16[128,2048]{1,0:T(8,128)(2,1)} %q_hbm.1, bf16[128,2048]{1,0:T(8,128)(2,1)} %k_hbm.1, bf16[128,2048]{1,0:T(8,128)(2,1)} %v_hbm.1, f32[16,128]{1,0:T(8,128)} %bitcast.3, f32[1,2048]{1,0:T(1,128)} %bitcast.4, bf16[2048,4096]{1,0:T(8,128)(2,1)} %w_hbm.1, s32[1,128]{1,0:T(1,128)} %bitcast.5, ...), custom_call_target="tpu_custom_call" | custom-call | flops 2147483648 | bytes 16777216 | tf_op jit(solution)/shard_map/pallas_call | solution.py:338
  36.1 1.9 %copy.10 = bf16[128,2048]{1,0:T(8,128)(2,1)} copy(bf16[128,2048]{1,0:T(8,128)(2,1)} %shard_map.82) | data formatting | bytes 1048576
